TPU v7x, 128 devices: a whole 4x4x4 slice. The times are simulated.
128 devices in a mesh: grp: 8 (over x, core), tie: 16 (over y, z).
Axes of the slice: x: 4, y: 4, z: 4, core: 2. Of those that a mesh axis runs over, the one named last changes fastest.
Arguments:
- soil_disp: bfloat16 [64, 32768], P(None, ('grp', 'tie')), may hold values from -6 to 6
- soil_vals: bfloat16 [7, 64, 64, 32768], P(None, None, None, ('grp', 'tie')), may hold values from -0.25 to 0.25
- soil_cols: int32 [7, 32768], P(None, ('grp', 'tie')), may hold values from 0 to 319, as said below
- load: float32 [64, 32768], P(None, ('grp', 'tie')), may hold values from -6 to 6
- pile_disp: bfloat16 [64, 131072], P(None, ('grp', 'tie')), may hold values from -6 to 6
- tie_vals: bfloat16 [64, 64, 131072], P(None, None, ('grp', 'tie')), may hold values from -0.75 to 0.75
- tie_pile: int32 [131072], P(('grp', 'tie')), may hold values from 0 to 16383, as said below
- tie_limit: float32 [131072], P(('grp', 'tie')), may hold values from 0.3 to 3
- tie_dest: int32 [131072], P(('grp', 'tie')), may hold values from 0 to 127, as said below
- tie_block: int32 [131072], P(('grp', 'tie')), may hold values from 0 to 255
Outputs:
- residual: float32 [64, 32768], P(None, ('grp', 'tie'))
Inputs may be any that keep to these rules, and one draw needn't show every extreme that they name: soil_cols[0, s] is 32 plus the block's own position on its device; the others lie within 32 blocks of it. On each device ties are listed by nondecreasing tie_dest; one device names one destination at most 16 times, and some destination is named exactly 16 times by every device. `tie_pile`: group segment q is held by the group's device q // 1024; the ties of one device name segments of one such device at most 128 times, and every device names some such device exactly 128 times.
All inputs are finite; a program needn't handle non-finite values.
Results may differ from a plain program's by a relative error of at most 0.0045.
Values may be sent and summed in bfloat16 or wider, within the bound.
A program may use at most 128 MiB of HBM per device.

v0:
```python
import jax
import jax.numpy as jnp
from jax import lax
from jax.sharding import PartitionSpec as P

RIM = 32


def extended(x, sides, width):
    for axis, dim in sides:
        count, length = (lax.axis_size(axis), x.shape[dim])
        up = [(i, (i + 1) % count) for i in range(count - 1)]
        down = [(j, i) for i, j in up]
        last = lax.slice_in_dim(x, length - width, length, axis=dim)
        first = lax.slice_in_dim(x, 0, width, axis=dim)
        before = lax.ppermute(last, axis, up)
        after = lax.ppermute(first, axis, down)
        x = jnp.concatenate([before, x, after], axis=dim)
    return x


def on_device(
    soil_disp,
    soil_vals,
    soil_cols,
    load,
    pile_disp,
    tie_vals,
    tie_pile,
    tie_limit,
    tie_dest,
    tie_block,
):
    blocks_here = soil_disp.shape[1]
    width = soil_disp.shape[0]
    wide = extended(soil_disp, ((("grp", "tie"), 1),), RIM)
    picked = wide[:, soil_cols]
    soil_image = jnp.einsum("kijb,jkb->ib", soil_vals, picked, preferred_element_type=jnp.float32)
    group_piles = lax.all_gather(pile_disp, "tie", axis=1, tiled=True)
    tie_states = group_piles[:, tie_pile]
    gap = jnp.einsum("ijt,jt->it", tie_vals, tie_states, preferred_element_type=jnp.float32)
    ratio = gap / tie_limit[None]
    force = (gap / jnp.sqrt(1.0 + ratio * ratio)).astype(jnp.bfloat16)
    owners = lax.axis_size(("grp", "tie"))
    target = tie_dest * blocks_here + tie_block
    term = (
        jnp.zeros((width, owners * blocks_here), jnp.float32)
        .at[:, target]
        .add(force.astype(jnp.float32))
    )
    tie_total = lax.psum_scatter(term, ("grp", "tie"), scatter_dimension=1, tiled=True)
    return soil_image + tie_total - load


def solution(mesh):
    return jax.shard_map(
        on_device,
        mesh=mesh,
        in_specs=(
            P(None, ("grp", "tie")),
            P(None, None, None, ("grp", "tie")),
            P(None, ("grp", "tie")),
            P(None, ("grp", "tie")),
            P(None, ("grp", "tie")),
            P(None, None, ("grp", "tie")),
            P(("grp", "tie")),
            P(("grp", "tie")),
            P(("grp", "tie")),
            P(("grp", "tie")),
        ),
        out_specs=P(None, ("grp", "tie")),
        check_vma=False,
    )
```

profile of v0, /device:TPU:0, one launch (start us, length us, event | category | flops | bytes accessed | tf_op | source)
XLA Modules:
  0.0 761.4 jit_solution(2425016110543405059)
XLA Ops:
  6.5 0.0 all-gather.2.cloned.1.call-start
  6.5 1.7 copy.20
  8.3 0.0 all-gather.2.cloned.1.call-update
  8.3 0.0 reduce-scatter.2.cloned.1.call-start
  8.3 0.7 fusion.7
  9.0 0.7 compare_select_fusion.2
  9.7 53.9 %all-gather.2.cloned.1.call-done = bf16[64,16384]{0,1:T(8,128)(2,1)} async-done(((bf16[64,1024]{0,1:T(8,128)(2,1)}), bf16[64,16384]{0,1:T(8,128)(2,1)}) %all-gather.2.cloned.1.call-update) | async-done | bytes 2097168 | tf_op jit(solution)/shard_map/all_gather | solution.py:39
  63.7 5.6 gather_fusion.1
  69.3 0.1 copy.38
  69.4 6.2 multiply_reduce_fusion.1
  75.6 0.7 convert_bitcast_fusion
  76.3 0.2 copy.21
  76.5 12.8 %scatter_custom_fusion = f32[64,32768]{0,1:T(8,128)} fusion(s32[1024]{0:T(1024)S(1)} %compare_select_fusion.2, f32[1024,64]{1,0:T(8,128)S(1)} %copy.21, f32[]{:T(128)} %constant.1.clone.1), kind=kCustom, calls=%fused_computation.5 | custom fusion | flops 65536 | bytes 8388612 | tf_op jit(solution)/shard_map/scatter-add | solution.py:49
  89.3 0.0 copy-start.1
  89.3 0.0 copy-start.2
  89.3 12.7 %copy.22 = f32[64,32768]{1,0:T(8,128)} copy(f32[64,32768]{0,1:T(8,128)} %scatter_custom_fusion) | data formatting | bytes 16777216 | tf_op jit(solution)/shard_map/scatter-add | solution.py:49
  102.0 0.0 copy-start
  102.0 0.0 reduce-scatter.2.cloned.1.call-update
  102.0 0.0 copy-done.1
  102.0 0.1 copy.17
  102.1 1.3 collective-permute-start.1
  103.4 4.7 collective-permute-start
  108.2 0.0 copy-done.2
  108.2 0.0 collective-permute-done.1
  108.2 1.1 collective-permute-done
  109.3 3.7 gather_fusion
  113.1 0.2 copy.37
  113.3 9.0 %multiply_reduce_fusion = f32[256,64]{0,1:T(8,128)S(1)} fusion(f32[256,64,7]{0,1,2:T(8,128)S(1)} %copy.37, bf16[7,64,64,256]{3,2,1,0:T(8,128)(2,1)} %param.11), kind=kLoop, calls=%fused_computation.3 | loop fusion | flops 22003712 | bytes 15204352 | tf_op jit(solution)/shard_map/kijb,jkb->ib/dot_general | solution.py:38
  122.3 630.8 %reduce-scatter.2.cloned.1.call-done = f32[64,256]{1,0:T(8,128)} async-done(((f32[64,32768]{1,0:T(8,128)}), f32[64,256]{1,0:T(8,128)}) %reduce-scatter.2.cloned.1.call-update) | async-done | bytes 65552 | tf_op jit(solution)/shard_map/reduce_scatter | solution.py:51
  753.1 0.0 copy-done
  753.1 1.5 fusion.6
  (5 shorter events, 0.0 us)
Async XLA Ops:
  6.5 57.1 %all-gather.2.cloned.1.call-start = ((), (), s32[]{:S(2)}) async-start(), calls=%async_computation.1 | async-start | bytes 4456448 | tf_op jit(solution)/shard_map/all_gather | solution.py:39
  8.3 744.8 %reduce-scatter.2.cloned.1.call-start = ((), (), s32[]{:S(2)}) async-start(), calls=%async_computation.2 | async-start | bytes 8454144 | tf_op jit(solution)/shard_map/reduce_scatter | solution.py:51
  89.3 12.7 %copy-start.1 = (bf16[64,256]{1,0:T(8,128)(2,1)S(1)}, bf16[64,256]{1,0:T(8,128)(2,1)}, u32[]{:S(2)}) copy-start(bf16[64,256]{1,0:T(8,128)(2,1)} %param.10) | copy-start | bytes 98308
  89.3 18.9 %copy-start.2 = (s32[7,256]{1,0:T(8,128)S(1)}, s32[7,256]{1,0:T(8,128)}, u32[]{:S(2)}) copy-start(s32[7,256]{1,0:T(8,128)} %param.12) | copy-start | bytes 21508
  102.0 651.1 %copy-start = (f32[64,256]{1,0:T(8,128)S(1)}, f32[64,256]{1,0:T(8,128)}, u32[]{:S(2)}) copy-start(f32[64,256]{1,0:T(8,128)} %param.13) | copy-start | bytes 196612
  102.1 6.1 collective-permute-start.1
  103.4 5.9 collective-permute-start
Sparse Core Ops, SparseCore 0:
  9.5 54.1 all-gather.1
  102.1 650.9 reduce-scatter.1
where the time goes:
time: 762 us; the launch traced here: 761 us
  waiting for transfers between devices  686 us (90%)
  other arithmetic  31.5 us (4%)
  local copies, waits for them, and re-layouts  24.4 us (3%)
  between operations  13.5 us (2%)
    reduce_scatter x1, waiting for transfers between devices, on_device(): lax.psum_scatter(term, ('grp', 'tie'), scatter_dimension=1, tiled=True)  631 us
    all_gather x1, waiting for transfers between devices, on_device(): group_piles = lax.all_gather(pile_disp, 'tie', axis=1, tiled=True)  53.9 us
  transfers between devices with their start and end apart: 4, of which 3 were waited for; matrix products, arithmetic and copies ran while one was open for 2% of the time, Pallas kernels for 0%

commit v1 on v0

v1 whole, which is shorter than its diff:
```python
import jax
import jax.numpy as jnp
from jax import lax
from jax.experimental import pallas as pl
from jax.experimental.pallas import tpu as pltpu
from jax.sharding import PartitionSpec as P

MESH = pl.DeviceIdType.MESH
F32, BF16, I32 = jnp.float32, jnp.bfloat16, jnp.int32
NT, NG = 16, 8
ND = NT * NG
PCAP, CAP = 128, 16
B = 64
T = 1024
L = 128
NC = T // L


def one_hot(cond):
    return jnp.where(cond, 1.0, 0.0).astype(BF16)


def iota(shape, dim):
    return lax.broadcasted_iota(I32, shape, dim)


def slots(ids, n, cap):
    before = iota((L, 2 * L), 0)
    now = iota((L, 2 * L), 1)
    tri = one_hot((before < now) | (now >= L))
    rows = [ids[c : c + 1, :] == iota((n, L), 0) for c in range(NC)]
    hot = jnp.concatenate([one_hot(r) for r in rows], axis=0)
    sums = jnp.dot(hot, tri, preferred_element_type=F32)
    run = jnp.zeros((n, L), F32)
    out = []
    for c in range(NC):
        part = sums[c * n : (c + 1) * n]
        rank = jnp.sum(jnp.where(rows[c], part[:, :L] + run, 0.0), axis=0, keepdims=True)
        out.append(ids[c : c + 1, :] * cap + rank.astype(I32))
        run = run + part[:, L:]
    return out


def kernel(
    soil_disp, soil_vals, soil_cols, load, pile_disp, tie_vals, tie_pile, tie_limit, tie_dest, tie_block,
    out,
    sd, sv, sc, ld, pd, tv, tp, tl, td, tb,
    hot_p, hot_d, ask, asked, answer, piles, state, force, send, got, rim, acc, image,
    in_sem, ask_s, ask_r, ans_s, ans_r, rim_s, rim_r, frc_s, frc_r, ready,
):
    g, t = lax.axis_index("grp"), lax.axis_index("tie")
    me = g * NT + t
    bar = pltpu.get_barrier_semaphore()

    def greet_tie(k, _):
        pl.semaphore_signal(bar, inc=1, device_id=(g, lax.rem(t + k, NT)), device_id_type=MESH)
        return 0

    def greet_grp(k, _):
        pl.semaphore_signal(bar, inc=1, device_id=(lax.rem(g + k, NG), t), device_id_type=MESH)
        return 0

    lax.fori_loop(1, NT, greet_tie, 0)
    lax.fori_loop(1, NG, greet_grp, 0)

    pairs = [
        (tie_pile, tp), (pile_disp, pd), (tie_dest, td), (tie_block, tb), (tie_limit, tl), (soil_disp, sd),
        (soil_cols, sc), (load, ld), (tie_vals, tv), (soil_vals, sv),
    ]
    loads = {}
    for n, (src, dst) in enumerate(pairs):
        copy = pltpu.make_async_copy(src, dst, in_sem.at[n])
        copy.start()
        loads[n] = copy

    loads[0].wait()
    ids = tp[...]
    holder = ids // T
    seg = ids - holder * T
    where = slots(holder, NT, PCAP)

    def fill_p(h, _):
        for c in range(NC):
            hot_p[h, :, c * L : (c + 1) * L] = one_hot((where[c] - h * PCAP) == iota((PCAP, L), 0))
        return 0

    lax.fori_loop(0, NT, fill_p, 0)
    hi = seg // 32
    lo = seg - hi * 32
    hi_row = jnp.concatenate([hi[c : c + 1, :] for c in range(NC)], axis=1).astype(F32)
    lo_row = jnp.concatenate([lo[c : c + 1, :] for c in range(NC)], axis=1).astype(F32)
    first = iota((16, T), 0)
    digits = jnp.where(first == 0, hi_row, jnp.where(first == 1, lo_row, 0.0)).astype(BF16)

    def fill_ask(q, _):
        named = lax.dot_general(
            digits, hot_p[pl.ds(q * 4, 4)].reshape(4 * PCAP, T), (((1,), (1,)), ((), ())), preferred_element_type=F32
        )
        number = (named[0:1] * 32.0 + named[1:2]).astype(I32)
        for h in range(4):
            ask[q * 4 + h] = jnp.broadcast_to(number[:, h * L : (h + 1) * L], (8, L))
        return 0

    lax.fori_loop(0, NT // 4, fill_ask, 0)

    pl.semaphore_wait(bar, NT - 1 + NG - 1)

    def ask_copy(k):
        h = lax.rem(t + k, NT)
        return pltpu.make_async_remote_copy(
            ask.at[h], asked.at[t], ask_s.at[k], ask_r.at[k], device_id=(g, h), device_id_type=MESH
        )

    def start_ask(k, _):
        ask_copy(k).start()
        return 0

    lax.fori_loop(1, NT, start_ask, 0)
    asked[t] = ask[t]

    def greet_again(k, _):
        pl.semaphore_signal(ready, inc=1, device_id=(lax.rem(g + k, NG), t), device_id_type=MESH)
        return 0

    lax.fori_loop(1, NG, greet_again, 0)

    loads[2].wait()
    goes = slots(td[...], ND, CAP)

    def fill_d(m, _):
        for c in range(NC):
            hot_d[pl.ds(m * L, L), c * L : (c + 1) * L] = one_hot((goes[c] - m * L) == iota((L, L), 0))
        return 0

    lax.fori_loop(0, ND * CAP // L, fill_d, 0)

    loads[1].wait()

    def wait_ask(k, _):
        ask_copy(k).wait()
        return 0

    lax.fori_loop(1, NT, wait_ask, 0)

    def answer_copy(k):
        r = lax.rem(t + k, NT)
        return pltpu.make_async_remote_copy(
            answer.at[r], piles.at[t], ans_s.at[k], ans_r.at[k], device_id=(g, r), device_id_type=MESH
        )

    for q in range(NT // 4):
        hots = []
        for n in range(4):
            r = lax.rem(t + q * 4 + n + 1, NT)
            hots.append(one_hot(asked[r][0:1, :] == iota((T, L), 0)))
        found = jnp.dot(pd[...], jnp.concatenate(hots, axis=1), preferred_element_type=F32).astype(BF16)
        for n in range(4):
            k = q * 4 + n + 1
            block = found[:, n * L : (n + 1) * L]
            if k < NT:
                answer[lax.rem(t + k, NT)] = block
                answer_copy(k).start()
            else:
                piles[t] = block

    pl.semaphore_wait(ready, NG - 1)
    loads[5].wait()
    right, left = lax.rem(me + 1, ND), lax.rem(me + ND - 1, ND)
    to_right = pltpu.make_async_remote_copy(
        sd.at[:, pl.ds(L, L)], rim.at[0], rim_s.at[0], rim_r.at[0],
        device_id=(right // NT, lax.rem(right, NT)), device_id_type=MESH,
    )
    to_left = pltpu.make_async_remote_copy(
        sd.at[:, pl.ds(0, L)], rim.at[1], rim_s.at[1], rim_r.at[1],
        device_id=(left // NT, lax.rem(left, NT)), device_id_type=MESH,
    )
    to_right.start()
    to_left.start()

    for q in range(NT // 4):
        for n in range(4):
            if q * 4 + n > 0:
                answer_copy(q * 4 + n).wait()
        held = [lax.rem(t + NT - (q * 4 + n), NT) for n in range(4)]
        left_side = jnp.concatenate([piles[h] for h in held], axis=1)
        right_side = jnp.concatenate([hot_p[h] for h in held], axis=0)
        part = jnp.dot(left_side, right_side, preferred_element_type=F32)
        state[...] = part if q == 0 else state[...] + part

    for n in (3, 4, 8):
        loads[n].wait()
    force[B:] = jnp.zeros((L - B, T), BF16)
    for c in range(NC):
        cols = slice(c * L, (c + 1) * L)
        x = state[:, cols]
        limit = tl[c : c + 1, :]

        def rows(i, _):
            at = pl.multiple_of(i * 16, 16)
            y = tv[pl.ds(at, 16), :, cols].astype(F32) * x[None]
            gap = jnp.sum(jnp.sum(y.reshape(16, 8, 8, L), axis=1), axis=1)
            ratio = gap / limit
            force[pl.ds(at, 16), cols] = (gap / jnp.sqrt(1.0 + ratio * ratio)).astype(BF16)
            return 0

        lax.fori_loop(0, B // 16, rows, 0)
        tail = jnp.where(iota((16, L), 0) == 0, tb[c : c + 1, :].astype(F32), 0.0)
        force[B : B + 16, cols] = tail.astype(BF16)

    for m, (low, high) in enumerate(((0, 512), (0, T), (0, T), (512, T))):
        packed = lax.dot_general(
            hot_d[m * 512 : (m + 1) * 512, low:high], force[:, low:high], (((1,), (1,)), ((), ())),
            preferred_element_type=F32,
        )
        send[m * 512 : (m + 1) * 512] = packed.astype(BF16)

    def force_copy(k):
        d = lax.rem(me + k, ND)
        return pltpu.make_async_remote_copy(
            send.at[pl.ds(pl.multiple_of(d * CAP, CAP), CAP)], got.at[pl.ds(pl.multiple_of(me * CAP, CAP), CAP)],
            frc_s, frc_r, device_id=(d // NT, lax.rem(d, NT)), device_id_type=MESH,
        )

    def start_force(k, _):
        force_copy(k).start()
        return 0

    lax.fori_loop(1, ND, start_force, 0)
    own = pl.ds(pl.multiple_of(me * CAP, CAP), CAP)
    got[own] = send[own]

    loads[6].wait()
    to_right.wait()
    to_left.wait()
    before = jnp.where(me == 0, 0.0, rim[0].astype(F32)).astype(BF16)
    after = jnp.where(me == ND - 1, 0.0, rim[1].astype(F32)).astype(BF16)
    wide = jnp.concatenate([before, sd[...], after], axis=1)
    loads[9].wait()
    for c in range(2):
        cols = slice(c * L, (c + 1) * L)
        near = wide[:, c * L : c * L + 3 * L]
        acc[...] = jnp.zeros_like(acc)
        for k in range(7):
            at = sc[k : k + 1, cols] + (96 - c * L)
            x = jnp.dot(near, one_hot(at == iota((3 * L, L), 0)), preferred_element_type=F32)

            def more(i, _, k=k, x=x, cols=cols):
                rows = pl.ds(pl.multiple_of(i * 16, 16), 16)
                y = sv[k, rows, :, cols].astype(F32) * x[None]
                acc[rows] = acc[rows] + jnp.sum(y.reshape(16, 8, 8, L), axis=1)
                return 0

            lax.fori_loop(0, B // 16, more, 0)
        image[:, cols] = jnp.sum(acc[...], axis=1)

    n = (ND - 1) * CAP
    pltpu.make_async_remote_copy(
        send.at[pl.ds(0, n)], got.at[pl.ds(0, n)], frc_s, frc_r, device_id=(g, t), device_id_type=MESH
    ).wait()
    loads[7].wait()
    block = got[:, B : B + 1].astype(F32).astype(I32)
    spread = one_hot(block == iota((ND * CAP, 256), 1))
    total = lax.dot_general(got[...], spread, (((0,), (0,)), ((), ())), preferred_element_type=F32)
    out[...] = image[...] + total[:B] - ld[...]


def on_device(
    soil_disp, soil_vals, soil_cols, load, pile_disp, tie_vals, tie_pile, tie_limit, tie_dest, tie_block
):
    lanes = [x.reshape(NC, L) for x in (tie_pile, tie_limit, tie_dest, tie_block)]
    args = [soil_disp, soil_vals, soil_cols, load, pile_disp, tie_vals, *lanes]
    dma = pltpu.SemaphoreType.DMA
    return pl.pallas_call(
        kernel,
        out_shape=jax.ShapeDtypeStruct(load.shape, F32),
        in_specs=[pl.BlockSpec(memory_space=pl.ANY)] * len(args),
        out_specs=pl.BlockSpec(memory_space=pltpu.VMEM),
        scratch_shapes=[
            *[pltpu.VMEM(x.shape, x.dtype) for x in args],
            pltpu.VMEM((NT, PCAP, T), BF16),
            pltpu.VMEM((ND * CAP, T), BF16),
            pltpu.VMEM((NT, 8, L), I32),
            pltpu.VMEM((NT, 8, L), I32),
            pltpu.VMEM((NT, B, L), BF16),
            pltpu.VMEM((NT, B, L), BF16),
            pltpu.VMEM((B, T), F32),
            pltpu.VMEM((L, T), BF16),
            pltpu.VMEM((ND * CAP, L), BF16),
            pltpu.VMEM((ND * CAP, L), BF16),
            pltpu.VMEM((2, B, L), BF16),
            pltpu.VMEM((B, 8, L), F32),
            pltpu.VMEM((B, 256), F32),
            dma((len(args),)),
            dma((NT,)), dma((NT,)), dma((NT,)), dma((NT,)), dma((2,)), dma((2,)), dma, dma,
            pltpu.SemaphoreType.REGULAR,
        ],
        compiler_params=pltpu.CompilerParams(
            collective_id=0, has_side_effects=True, vmem_limit_bytes=56 * 1024 * 1024
        ),
        cost_estimate=pl.CostEstimate(flops=3_000_000_000, bytes_accessed=24_000_000, transcendentals=65536),
        name="residual",
    )(*args)


def solution(mesh):
    both = ("grp", "tie")
    return jax.shard_map(
        on_device,
        mesh=mesh,
        in_specs=(
            P(None, both), P(None, None, None, both), P(None, both), P(None, both), P(None, both),
            P(None, None, both), P(both), P(both), P(both), P(both),
        ),
        out_specs=P(None, both),
        check_vma=False,
    )
```

time: 762 us -> 39.3 us (0.05)
  the two profiles are of different devices: /device:TPU:0 before, /device:TPU:1 now
where the time goes in v1:
time: 39.3 us; the launch traced here: 39.1 us
  Pallas kernels  37.6 us (96%)
  local copies, waits for them, and re-layouts  1.47 us (4%)
    pallas_call x1, Pallas kernels, on_device(): pl.pallas_call(kernel, out_shape=jax.ShapeDtypeStruct(load.shape, F32), i...  37.6 us
    unnamed x1, local copies, waits for them, and re-layouts  1.47 us

profile of v1, /device:TPU:1, one launch (start us, length us, event | category | flops | bytes accessed | tf_op | source)
XLA Modules:
  0.0 39.1 jit_solution(2281788014102799839)
XLA Ops:
  0.0 37.6 %residual.1 = f32[64,256]{1,0:T(8,128)} custom-call(bf16[64,256]{1,0:T(8,128)(2,1)} %soil_disp.1, bf16[7,64,64,256]{3,2,1,0:T(8,128)(2,1)} %soil_vals.1, s32[7,256]{1,0:T(8,128)} %soil_cols.1, f32[64,256]{1,0:T(8,128)} %load.1, bf16[64,1024]{1,0:T(8,128)(2,1)} %pile_disp.1, bf16[64,64,1024]{2,1,0:T(8,128)(2,1)} %tie_vals.1, s32[8,128]{1,0:T(8,128)} %bitcast.4, ...), custom_call_target="tpu_custom_call" | custom-call | flops 3000000000 | bytes 24000000 | tf_op jit(solution)/shard_map/residual/pallas_call | solution.py:273
  37.6 1.5 %copy.12 = f32[64,256]{1,0:T(8,128)} copy(f32[64,256]{1,0:T(8,128)} %residual.1) | data formatting | bytes 131072

commit v2 on v1

--- a/solution.py
+++ b/solution.py
@@ -45,7 +45,7 @@
     soil_disp, soil_vals, soil_cols, load, pile_disp, tie_vals, tie_pile, tie_limit, tie_dest, tie_block,
     out,
     sd, sv, sc, ld, pd, tv, tp, tl, td, tb,
-    hot_p, hot_d, ask, asked, answer, piles, state, force, send, got, rim, acc, image,
+    hot_p, hot_d, ask, asked, answer, piles, state, force, slotted, send, got, rim, acc, image,
     in_sem, ask_s, ask_r, ans_s, ans_r, rim_s, rim_r, frc_s, frc_r, ready,
 ):
     g, t = lax.axis_index("grp"), lax.axis_index("tie")
@@ -65,8 +65,10 @@
 
     pairs = [
         (tie_pile, tp), (pile_disp, pd), (tie_dest, td), (tie_block, tb), (tie_limit, tl), (soil_disp, sd),
-        (soil_cols, sc), (load, ld), (tie_vals, tv), (soil_vals, sv),
+        (soil_cols, sc), (load, ld),
     ]
+    pairs += [(tie_vals.at[:, :, pl.ds(c * L, L)], tv.at[c]) for c in range(NC)]
+    pairs += [(soil_vals.at[:, :, :, pl.ds(c * L, L)], sv.at[c]) for c in range(2)]
     loads = {}
     for n, (src, dst) in enumerate(pairs):
         copy = pltpu.make_async_copy(src, dst, in_sem.at[n])
@@ -98,7 +100,7 @@
         )
         number = (named[0:1] * 32.0 + named[1:2]).astype(I32)
         for h in range(4):
-            ask[q * 4 + h] = jnp.broadcast_to(number[:, h * L : (h + 1) * L], (8, L))
+            ask[q * 4 + h] = number[:, h * L : (h + 1) * L]
         return 0
 
     lax.fori_loop(0, NT // 4, fill_ask, 0)
@@ -136,12 +138,6 @@
 
     loads[1].wait()
 
-    def wait_ask(k, _):
-        ask_copy(k).wait()
-        return 0
-
-    lax.fori_loop(1, NT, wait_ask, 0)
-
     def answer_copy(k):
         r = lax.rem(t + k, NT)
         return pltpu.make_async_remote_copy(
@@ -151,8 +147,10 @@
     for q in range(NT // 4):
         hots = []
         for n in range(4):
+            if q * 4 + n + 1 < NT:
+                ask_copy(NT - (q * 4 + n + 1)).wait()
             r = lax.rem(t + q * 4 + n + 1, NT)
-            hots.append(one_hot(asked[r][0:1, :] == iota((T, L), 0)))
+            hots.append(one_hot(asked[r] == iota((T, L), 0)))
         found = jnp.dot(pd[...], jnp.concatenate(hots, axis=1), preferred_element_type=F32).astype(BF16)
         for n in range(4):
             k = q * 4 + n + 1
@@ -187,32 +185,33 @@
         part = jnp.dot(left_side, right_side, preferred_element_type=F32)
         state[...] = part if q == 0 else state[...] + part
 
-    for n in (3, 4, 8):
-        loads[n].wait()
-    force[B:] = jnp.zeros((L - B, T), BF16)
+    loads[3].wait()
+    loads[4].wait()
     for c in range(NC):
         cols = slice(c * L, (c + 1) * L)
-        x = state[:, cols]
-        limit = tl[c : c + 1, :]
-
-        def rows(i, _):
-            at = pl.multiple_of(i * 16, 16)
-            y = tv[pl.ds(at, 16), :, cols].astype(F32) * x[None]
-            gap = jnp.sum(jnp.sum(y.reshape(16, 8, 8, L), axis=1), axis=1)
-            ratio = gap / limit
-            force[pl.ds(at, 16), cols] = (gap / jnp.sqrt(1.0 + ratio * ratio)).astype(BF16)
-            return 0
-
-        lax.fori_loop(0, B // 16, rows, 0)
-        tail = jnp.where(iota((16, L), 0) == 0, tb[c : c + 1, :].astype(F32), 0.0)
-        force[B : B + 16, cols] = tail.astype(BF16)
-
-    for m, (low, high) in enumerate(((0, 512), (0, T), (0, T), (512, T))):
-        packed = lax.dot_general(
-            hot_d[m * 512 : (m + 1) * 512, low:high], force[:, low:high], (((1,), (1,)), ((), ())),
-            preferred_element_type=F32,
-        )
-        send[m * 512 : (m + 1) * 512] = packed.astype(BF16)
+        x = state[:, cols].astype(BF16)
+        loads[8 + c].wait()
+        for i in range(0, B, 16):
+            y = tv[c, i : i + 16] * x[None]
+            y = (y[:, :32] + y[:, 32:]).astype(F32)
+            gap = jnp.sum(jnp.sum(y.reshape(16, 4, 8, L), axis=1), axis=1)
+            ratio = gap / tl[c : c + 1, :]
+            force[i : i + 16, cols] = (gap / jnp.sqrt(1.0 + ratio * ratio)).astype(BF16)
+        tail = jnp.where(iota((B, L), 0) == 0, tb[c : c + 1, :].astype(F32), 0.0)
+        force[B:, cols] = tail.astype(BF16)
+        if c % 2:
+            low = (c - 1) * L
+            pair = slice(low, low + 2 * L)
+            packed = lax.dot_general(
+                hot_d[low : low + T + 2 * L, pair], force[:, pair], (((1,), (1,)), ((), ())), preferred_element_type=F32
+            )
+            if c == 1:
+                slotted[: T + 2 * L] = packed
+            else:
+                slotted[low : low + T] = slotted[low : low + T] + packed[:T]
+                slotted[low + T : low + T + 2 * L] = packed[T:]
+    for m in range(0, ND * CAP, 512):
+        send[m : m + 512] = slotted[m : m + 512].astype(BF16)
 
     def force_copy(k):
         d = lax.rem(me + k, ND)
@@ -235,8 +234,8 @@
     before = jnp.where(me == 0, 0.0, rim[0].astype(F32)).astype(BF16)
     after = jnp.where(me == ND - 1, 0.0, rim[1].astype(F32)).astype(BF16)
     wide = jnp.concatenate([before, sd[...], after], axis=1)
-    loads[9].wait()
     for c in range(2):
+        loads[8 + NC + c].wait()
         cols = slice(c * L, (c + 1) * L)
         near = wide[:, c * L : c * L + 3 * L]
         acc[...] = jnp.zeros_like(acc)
@@ -244,9 +243,9 @@
             at = sc[k : k + 1, cols] + (96 - c * L)
             x = jnp.dot(near, one_hot(at == iota((3 * L, L), 0)), preferred_element_type=F32)
 
-            def more(i, _, k=k, x=x, cols=cols):
+            def more(i, _, c=c, k=k, x=x):
                 rows = pl.ds(pl.multiple_of(i * 16, 16), 16)
-                y = sv[k, rows, :, cols].astype(F32) * x[None]
+                y = sv[c, k, rows].astype(F32) * x[None]
                 acc[rows] = acc[rows] + jnp.sum(y.reshape(16, 8, 8, L), axis=1)
                 return 0
 
@@ -269,6 +268,7 @@
 ):
     lanes = [x.reshape(NC, L) for x in (tie_pile, tie_limit, tie_dest, tie_block)]
     args = [soil_disp, soil_vals, soil_cols, load, pile_disp, tie_vals, *lanes]
+    tiles = {1: (2, 7, B, B, L), 5: (NC, B, B, L)}
     dma = pltpu.SemaphoreType.DMA
     return pl.pallas_call(
         kernel,
@@ -276,21 +276,22 @@
         in_specs=[pl.BlockSpec(memory_space=pl.ANY)] * len(args),
         out_specs=pl.BlockSpec(memory_space=pltpu.VMEM),
         scratch_shapes=[
-            *[pltpu.VMEM(x.shape, x.dtype) for x in args],
+            *[pltpu.VMEM(tiles.get(n, x.shape), x.dtype) for n, x in enumerate(args)],
             pltpu.VMEM((NT, PCAP, T), BF16),
             pltpu.VMEM((ND * CAP, T), BF16),
-            pltpu.VMEM((NT, 8, L), I32),
-            pltpu.VMEM((NT, 8, L), I32),
+            pltpu.VMEM((NT, 1, L), I32),
+            pltpu.VMEM((NT, 1, L), I32),
             pltpu.VMEM((NT, B, L), BF16),
             pltpu.VMEM((NT, B, L), BF16),
             pltpu.VMEM((B, T), F32),
             pltpu.VMEM((L, T), BF16),
+            pltpu.VMEM((ND * CAP, L), F32),
             pltpu.VMEM((ND * CAP, L), BF16),
             pltpu.VMEM((ND * CAP, L), BF16),
             pltpu.VMEM((2, B, L), BF16),
             pltpu.VMEM((B, 8, L), F32),
             pltpu.VMEM((B, 256), F32),
-            dma((len(args),)),
+            dma((8 + NC + 2,)),
             dma((NT,)), dma((NT,)), dma((NT,)), dma((NT,)), dma((2,)), dma((2,)), dma, dma,
             pltpu.SemaphoreType.REGULAR,
         ],

time: 39.3 us -> 36.6 us (0.931)
  Pallas kernels: 37.6 us -> 35 us
    pallas_call x1, Pallas kernels: 37.6 us -> 35 us  [on_device(): pl.pallas_call(kernel, out_shape=jax.ShapeDtypeStruct(load.shape, F32), i...]
where the time goes in v2:
time: 36.6 us; the launch traced here: 36.5 us
  Pallas kernels  35 us (96%)
  local copies, waits for them, and re-layouts  1.47 us (4%)
    pallas_call x1, Pallas kernels, on_device(): pl.pallas_call(kernel, out_shape=jax.ShapeDtypeStruct(load.shape, F32), i...  35 us
    unnamed x1, local copies, waits for them, and re-layouts  1.47 us

profile of v2, /device:TPU:1, one launch (start us, length us, event | category | flops | bytes accessed | tf_op | source)
XLA Modules:
  0.0 36.5 jit_solution(9627706082916604430)
XLA Ops:
  0.0 35.0 %residual.1 = f32[64,256]{1,0:T(8,128)} custom-call(bf16[64,256]{1,0:T(8,128)(2,1)} %soil_disp.1, bf16[7,64,64,256]{3,2,1,0:T(8,128)(2,1)} %soil_vals.1, s32[7,256]{1,0:T(8,128)} %soil_cols.1, f32[64,256]{1,0:T(8,128)} %load.1, bf16[64,1024]{1,0:T(8,128)(2,1)} %pile_disp.1, bf16[64,64,1024]{2,1,0:T(8,128)(2,1)} %tie_vals.1, s32[8,128]{1,0:T(8,128)} %bitcast.4, ...), custom_call_target="tpu_custom_call" | custom-call | flops 3000000000 | bytes 24000000 | tf_op jit(solution)/shard_map/residual/pallas_call | solution.py:273
  35.0 1.5 %copy.12 = f32[64,256]{1,0:T(8,128)} copy(f32[64,256]{1,0:T(8,128)} %residual.1) | data formatting | bytes 131072

commit v3 on v2

--- a/solution.py
+++ b/solution.py
@@ -187,46 +187,49 @@
 
     loads[3].wait()
     loads[4].wait()
+    slotted[...] = jnp.zeros_like(slotted)
+    force[B:] = jnp.zeros((B, T), BF16)
     for c in range(NC):
-        cols = slice(c * L, (c + 1) * L)
-        x = state[:, cols].astype(BF16)
+        force[B : B + 16, c * L : (c + 1) * L] = jnp.where(
+            iota((16, L), 0) == 0, tb[c : c + 1, :].astype(F32), 0.0
+        ).astype(BF16)
         loads[8 + c].wait()
-        for i in range(0, B, 16):
-            y = tv[c, i : i + 16] * x[None]
-            y = (y[:, :32] + y[:, 32:]).astype(F32)
-            gap = jnp.sum(jnp.sum(y.reshape(16, 4, 8, L), axis=1), axis=1)
-            ratio = gap / tl[c : c + 1, :]
-            force[i : i + 16, cols] = (gap / jnp.sqrt(1.0 + ratio * ratio)).astype(BF16)
-        tail = jnp.where(iota((B, L), 0) == 0, tb[c : c + 1, :].astype(F32), 0.0)
-        force[B:, cols] = tail.astype(BF16)
-        if c % 2:
-            low = (c - 1) * L
-            pair = slice(low, low + 2 * L)
-            packed = lax.dot_general(
-                hot_d[low : low + T + 2 * L, pair], force[:, pair], (((1,), (1,)), ((), ())), preferred_element_type=F32
-            )
-            if c == 1:
-                slotted[: T + 2 * L] = packed
-            else:
-                slotted[low : low + T] = slotted[low : low + T] + packed[:T]
-                slotted[low + T : low + T + 2 * L] = packed[T:]
-    for m in range(0, ND * CAP, 512):
-        send[m : m + 512] = slotted[m : m + 512].astype(BF16)
+
+    def two_columns(p, _):
+        for n in range(2):
+            c = p * 2 + n
+            cols = pl.ds(pl.multiple_of(c * L, L), L)
+            x = state[:, cols].astype(BF16)
+            for i in range(0, B, 16):
+                y = tv[c, i : i + 16] * x[None]
+                y = (y[:, :32] + y[:, 32:]).astype(F32)
+                gap = jnp.sum(jnp.sum(y.reshape(16, 4, 8, L), axis=1), axis=1)
+                ratio = gap / tl[pl.ds(c, 1), :]
+                force[i : i + 16, cols] = (gap / jnp.sqrt(1.0 + ratio * ratio)).astype(BF16)
+        low = pl.multiple_of(p * 2 * L, 2 * L)
+        pair = pl.ds(low, 2 * L)
+        into = pl.ds(low, T + 2 * L)
+        slotted[into] = slotted[into] + lax.dot_general(
+            hot_d[into, pair], force[:, pair], (((1,), (1,)), ((), ())), preferred_element_type=F32
+        )
+        return 0
+
+    lax.fori_loop(0, NC // 2, two_columns, 0)
+    send[...] = slotted[...].astype(BF16)
 
     def force_copy(k):
         d = lax.rem(me + k, ND)
         return pltpu.make_async_remote_copy(
-            send.at[pl.ds(pl.multiple_of(d * CAP, CAP), CAP)], got.at[pl.ds(pl.multiple_of(me * CAP, CAP), CAP)],
-            frc_s, frc_r, device_id=(d // NT, lax.rem(d, NT)), device_id_type=MESH,
+            send.at[pl.ds(pl.multiple_of(d * CAP, CAP), CAP)], got.at[pl.ds(pl.multiple_of(k * CAP, CAP), CAP)],
+            frc_s, frc_r.at[k // 32], device_id=(d // NT, lax.rem(d, NT)), device_id_type=MESH,
         )
 
     def start_force(k, _):
         force_copy(k).start()
         return 0
 
-    lax.fori_loop(1, ND, start_force, 0)
-    own = pl.ds(pl.multiple_of(me * CAP, CAP), CAP)
-    got[own] = send[own]
+    lax.fori_loop(1, ND, start_force, 0, unroll=True)
+    got[:CAP] = send[pl.ds(pl.multiple_of(me * CAP, CAP), CAP)]
 
     loads[6].wait()
     to_right.wait()
@@ -238,29 +241,38 @@
         loads[8 + NC + c].wait()
         cols = slice(c * L, (c + 1) * L)
         near = wide[:, c * L : c * L + 3 * L]
-        acc[...] = jnp.zeros_like(acc)
         for k in range(7):
             at = sc[k : k + 1, cols] + (96 - c * L)
-            x = jnp.dot(near, one_hot(at == iota((3 * L, L), 0)), preferred_element_type=F32)
-
-            def more(i, _, c=c, k=k, x=x):
-                rows = pl.ds(pl.multiple_of(i * 16, 16), 16)
-                y = sv[c, k, rows].astype(F32) * x[None]
-                acc[rows] = acc[rows] + jnp.sum(y.reshape(16, 8, 8, L), axis=1)
-                return 0
-
-            lax.fori_loop(0, B // 16, more, 0)
-        image[:, cols] = jnp.sum(acc[...], axis=1)
-
+            picked = jnp.dot(near, one_hot(at == iota((3 * L, L), 0)), preferred_element_type=F32)
+            acc[k] = picked.astype(BF16)
+
+        def more(i, _, c=c, cols=cols):
+            some = pl.ds(pl.multiple_of(i * 8, 8), 8)
+            total = jnp.zeros((8, 8, L), F32)
+            for k in range(7):
+                y = sv[c, k, some] * acc[k][None]
+                y = (y[:, :32] + y[:, 32:]).astype(F32)
+                total = total + jnp.sum(y.reshape(8, 4, 8, L), axis=1)
+            image[some, cols] = jnp.sum(total, axis=1)
+            return 0
+
+        lax.fori_loop(0, B // 8, more, 0, unroll=2)
+
+    loads[7].wait()
+    total = image[...] - ld[...]
+    for j in range(4):
+        n = 32 * CAP - (CAP if j == 0 else 0)
+        pltpu.make_async_remote_copy(
+            send.at[pl.ds(0, n)], got.at[pl.ds(0, n)], frc_s, frc_r.at[j], device_id=(g, t), device_id_type=MESH
+        ).wait_recv()
+        part = got[j * 32 * CAP : (j + 1) * 32 * CAP]
+        spread = one_hot(part[:, B : B + 1].astype(F32).astype(I32) == iota((32 * CAP, 256), 1))
+        total = total + lax.dot_general(part, spread, (((0,), (0,)), ((), ())), preferred_element_type=F32)[:B]
+    out[...] = total
     n = (ND - 1) * CAP
     pltpu.make_async_remote_copy(
-        send.at[pl.ds(0, n)], got.at[pl.ds(0, n)], frc_s, frc_r, device_id=(g, t), device_id_type=MESH
-    ).wait()
-    loads[7].wait()
-    block = got[:, B : B + 1].astype(F32).astype(I32)
-    spread = one_hot(block == iota((ND * CAP, 256), 1))
-    total = lax.dot_general(got[...], spread, (((0,), (0,)), ((), ())), preferred_element_type=F32)
-    out[...] = image[...] + total[:B] - ld[...]
+        send.at[pl.ds(0, n)], got.at[pl.ds(0, n)], frc_s, frc_r.at[0], device_id=(g, t), device_id_type=MESH
+    ).wait_send()
 
 
 def on_device(
@@ -289,10 +301,10 @@
             pltpu.VMEM((ND * CAP, L), BF16),
             pltpu.VMEM((ND * CAP, L), BF16),
             pltpu.VMEM((2, B, L), BF16),
-            pltpu.VMEM((B, 8, L), F32),
+            pltpu.VMEM((7, B, L), BF16),
             pltpu.VMEM((B, 256), F32),
             dma((8 + NC + 2,)),
-            dma((NT,)), dma((NT,)), dma((NT,)), dma((NT,)), dma((2,)), dma((2,)), dma, dma,
+            dma((NT,)), dma((NT,)), dma((NT,)), dma((NT,)), dma((2,)), dma((2,)), dma, dma((4,)),
             pltpu.SemaphoreType.REGULAR,
         ],
         compiler_params=pltpu.CompilerParams(

time: 36.6 us -> 36.4 us (level)
  no operation moved by 1% of the time
where the time goes in v3:
time: 36.4 us; the launch traced here: 36.3 us
  Pallas kernels  34.8 us (96%)
  local copies, waits for them, and re-layouts  1.47 us (4%)
    pallas_call x1, Pallas kernels, on_device(): pl.pallas_call(kernel, out_shape=jax.ShapeDtypeStruct(load.shape, F32), i...  34.8 us
    unnamed x1, local copies, waits for them, and re-layouts  1.47 us

profile of v3, /device:TPU:1, one launch (start us, length us, event | category | flops | bytes accessed | tf_op | source)
XLA Modules:
  0.0 36.3 jit_solution(11568735834564259654)
XLA Ops:
  0.0 34.8 %residual.1 = f32[64,256]{1,0:T(8,128)} custom-call(bf16[64,256]{1,0:T(8,128)(2,1)} %soil_disp.1, bf16[7,64,64,256]{3,2,1,0:T(8,128)(2,1)} %soil_vals.1, s32[7,256]{1,0:T(8,128)} %soil_cols.1, f32[64,256]{1,0:T(8,128)} %load.1, bf16[64,1024]{1,0:T(8,128)(2,1)} %pile_disp.1, bf16[64,64,1024]{2,1,0:T(8,128)(2,1)} %tie_vals.1, s32[8,128]{1,0:T(8,128)} %bitcast.4, ...), custom_call_target="tpu_custom_call" | custom-call | flops 3000000000 | bytes 24000000 | tf_op jit(solution)/shard_map/residual/pallas_call | solution.py:285
  34.8 1.5 %copy.12 = f32[64,256]{1,0:T(8,128)} copy(f32[64,256]{1,0:T(8,128)} %residual.1) | data formatting | bytes 131072

commit v4 on v3

--- a/solution.py
+++ b/solution.py
@@ -250,9 +250,8 @@
             some = pl.ds(pl.multiple_of(i * 8, 8), 8)
             total = jnp.zeros((8, 8, L), F32)
             for k in range(7):
-                y = sv[c, k, some] * acc[k][None]
-                y = (y[:, :32] + y[:, 32:]).astype(F32)
-                total = total + jnp.sum(y.reshape(8, 4, 8, L), axis=1)
+                y = sv[c, k, some].astype(F32) * acc[k].astype(F32)[None]
+                total = total + jnp.sum(y.reshape(8, 8, 8, L), axis=1)
             image[some, cols] = jnp.sum(total, axis=1)
             return 0
 

time: 36.4 us -> 36.4 us (level)
  no operation moved by 1% of the time
where the time goes in v4:
time: 36.4 us; the launch traced here: 36.3 us
  Pallas kernels  34.8 us (96%)
  local copies, waits for them, and re-layouts  1.47 us (4%)
    pallas_call x1, Pallas kernels, on_device(): pl.pallas_call(kernel, out_shape=jax.ShapeDtypeStruct(load.shape, F32), i...  34.8 us
    unnamed x1, local copies, waits for them, and re-layouts  1.47 us

profile of v4, /device:TPU:1, one launch (start us, length us, event | category | flops | bytes accessed | tf_op | source)
XLA Modules:
  0.0 36.3 jit_solution(1613915421694977064)
XLA Ops:
  0.0 34.8 %residual.1 = f32[64,256]{1,0:T(8,128)} custom-call(bf16[64,256]{1,0:T(8,128)(2,1)} %soil_disp.1, bf16[7,64,64,256]{3,2,1,0:T(8,128)(2,1)} %soil_vals.1, s32[7,256]{1,0:T(8,128)} %soil_cols.1, f32[64,256]{1,0:T(8,128)} %load.1, bf16[64,1024]{1,0:T(8,128)(2,1)} %pile_disp.1, bf16[64,64,1024]{2,1,0:T(8,128)(2,1)} %tie_vals.1, s32[8,128]{1,0:T(8,128)} %bitcast.4, ...), custom_call_target="tpu_custom_call" | custom-call | flops 3000000000 | bytes 24000000 | tf_op jit(solution)/shard_map/residual/pallas_call | solution.py:284
  34.8 1.5 %copy.12 = f32[64,256]{1,0:T(8,128)} copy(f32[64,256]{1,0:T(8,128)} %residual.1) | data formatting | bytes 131072
